TPU v7x, 256 devices: a whole 4x4x8 slice. The times are simulated.
256 devices in a mesh: dp: 32 (over z, x), seq: 8 (over y, core).
Axes of the slice: x: 4, y: 4, z: 8, core: 2. Of those that a mesh axis runs over, the one named last changes fastest.
Arguments:
- patches: bfloat16 [32, 98304], P(None, ('dp', 'seq')), may hold values from -12 to 12
- segment_ids: int32 [32, 3072], P('dp'), may hold values from 0 to 15, never falling along the last dimension, each value on 1 to 2304 neighbouring positions
- regroup_plan: int32 [32, 5, 64], P('dp'), may hold values from 0 to 383, as said below
- input_weight: bfloat16 [32, 1280], replicated, may hold values from -1 to 1
- input_bias: float32 [1280], replicated, may hold values from -3 to 3
- skip_weight: bfloat16 [32, 1280], replicated, may hold values from -1 to 1
- hidden_weight: bfloat16 [1280, 1280], replicated, may hold values from -0.15625 to 0.15625
- output_bias: float32 [1280], replicated, may hold values from -3 to 3
- norm_gain: float32 [1280], replicated, may hold values from 0.1 to 1.9
- head_scale: float32 [8], replicated, may hold values from 1 to 4
- qkv_weight: bfloat16 [1280, 3, 640], replicated, may hold values from -0.15625 to 0.15625
- out_weight: bfloat16 [640, 1280], P(None, ('dp', 'seq')), may hold values from -0.25 to 0.25
- cotangent: bfloat16 [98304, 1280], P(('dp', 'seq')), may hold values from -0.3125 to 0.3125
Outputs:
- layer_out: bfloat16 [98304, 1280], P(('dp', 'seq'))
- out_grad: float32 [640, 1280], P(None, ('dp', 'seq'))
Inputs may be any that keep to these rules, and one draw needn't show every extreme that they name: `regroup_plan`: piece s * 8 + d of a window moves rows of source shard s to destination shard d: one piece for each pair, each moving one row or more. The pieces of a window cover each of the 384 rows of every source shard once and each of the 384 rows of every destination shard once. A piece moves at most 96 rows, and in every window some piece moves exactly 96. `segment_ids`: series ids never fall along a window's positions; one series of each window has exactly 2304 positions.
All inputs are finite; a program needn't handle non-finite values.
Results may differ from a plain program's by a relative error of at most 0.015.
Values may be sent and summed in bfloat16 or wider, within the bound.
A program may use at most 64 MiB of HBM per device.

v0:
```python
import math
import jax
import jax.numpy as jnp
from jax import lax
from jax.sharding import PartitionSpec as P

HD = 80
EPSILON = 1e-06
CONTRACT_FIRST = (((0,), (0,)), ((), ()))


def row_norm(values):
    return values * lax.rsqrt(jnp.mean(values * values, axis=-1, keepdims=True) + EPSILON)


def place_table(plan_rows, shard_rows, shard_count):
    source = plan_rows[0]
    first_row = plan_rows[1]
    row_count = plan_rows[2]
    target = plan_rows[3]
    offset_row = plan_rows[4]
    window_len = shard_rows * shard_count
    loader_row = jnp.arange(window_len, dtype=jnp.int32)
    begin_row = source * shard_rows + first_row
    inside = (loader_row[None, :] >= begin_row[:, None]) & (
        loader_row[None, :] < (begin_row + row_count)[:, None]
    )
    earlier = (
        (source[:, None] == source[None, :])
        & (target[:, None] == target[None, :])
        & (first_row[None, :] < first_row[:, None])
    )
    base_rank = jnp.sum(jnp.where(earlier, row_count[None, :], 0), axis=1)
    position = jnp.sum(
        jnp.where(
            inside, (target * shard_rows + offset_row - begin_row)[:, None] + loader_row[None, :], 0
        ),
        axis=0,
    )
    slot_rank = jnp.sum(
        jnp.where(inside, (base_rank - begin_row)[:, None] + loader_row[None, :], 0), axis=0
    )
    return (position, slot_rank)


def patch_block(columns, input_weight, input_bias, skip_weight, hidden_weight, output_bias):
    pre_act = (
        lax.dot_general(columns, input_weight, CONTRACT_FIRST, preferred_element_type=jnp.float32)
        + input_bias
    )
    hidden = jax.nn.silu(pre_act).astype(jnp.bfloat16)
    skipped = lax.dot_general(
        columns, skip_weight, CONTRACT_FIRST, preferred_element_type=jnp.float32
    )
    embedded = (
        jnp.dot(hidden, hidden_weight, preferred_element_type=jnp.float32) + skipped + output_bias
    )
    return embedded.astype(jnp.bfloat16)


def per_device(
    patches,
    segment_ids,
    regroup_plan,
    input_weight,
    input_bias,
    skip_weight,
    hidden_weight,
    output_bias,
    norm_gain,
    head_scale,
    qkv_weight,
    out_weight,
    cotangent,
):
    shard_count = lax.axis_size("seq")
    shard_index = lax.axis_index("seq")
    shard_rows = cotangent.shape[0]
    model_width = cotangent.shape[1]
    window_len = shard_rows * shard_count
    capacity = 2 * shard_rows // shard_count
    position, slot_rank = place_table(regroup_plan[0], shard_rows, shard_count)
    loader_row = jnp.arange(window_len, dtype=jnp.int32)
    own_rows = lax.dynamic_slice_in_dim(position, shard_index * shard_rows, shard_rows, 0)
    own_ranks = lax.dynamic_slice_in_dim(slot_rank, shard_index * shard_rows, shard_rows, 0)
    send_slot = own_rows // shard_rows * capacity + own_ranks
    send_table = (
        jnp.full((shard_count * capacity,), shard_rows, jnp.int32)
        .at[send_slot]
        .set(jnp.arange(shard_rows, dtype=jnp.int32))
    )
    landing = jnp.where(position // shard_rows == shard_index, position % shard_rows, shard_rows)
    receive_table = (
        jnp.zeros((shard_rows,), jnp.int32)
        .at[landing]
        .set(loader_row // shard_rows * capacity + slot_rank, mode="drop")
    )
    local_embed = patch_block(
        patches, input_weight, input_bias, skip_weight, hidden_weight, output_bias
    )
    padded = jnp.concatenate([local_embed, jnp.zeros((1, model_width), jnp.bfloat16)], axis=0)
    arrived = lax.all_to_all(padded[send_table], "seq", split_axis=0, concat_axis=0, tiled=True)
    embedded = arrived[receive_table]
    normed = (row_norm(embedded.astype(jnp.float32)) * norm_gain).astype(jnp.bfloat16)
    projected = jnp.dot(
        normed, qkv_weight.reshape(model_width, -1), preferred_element_type=jnp.float32
    )
    projected = projected.astype(jnp.bfloat16).reshape(shard_rows, 3, -1)
    head_rows = lax.all_to_all(projected, "seq", split_axis=2, concat_axis=0, tiled=True)
    local_width = head_rows.shape[2]
    local_heads = local_width // HD
    queries = row_norm(
        head_rows[:, 0].reshape(window_len, local_heads, HD).astype(jnp.float32)
    ).astype(jnp.bfloat16)
    key_rows = row_norm(
        head_rows[:, 1].reshape(window_len, local_heads, HD).astype(jnp.float32)
    ).astype(jnp.bfloat16)
    value_rows = head_rows[:, 2].reshape(window_len, local_heads, HD)
    factor = lax.dynamic_slice_in_dim(head_scale, shard_index * local_heads, local_heads, 0) * (
        1.0 / math.sqrt(HD)
    )
    segment_row = segment_ids[0]
    block_len = min(512, window_len)
    block_count = window_len // block_len
    pieces = []
    for block_index in range(block_count):
        query_first = block_index * block_len
        query_part = queries[query_first : query_first + block_len]
        query_pos = query_first + jnp.arange(block_len, dtype=jnp.int32)
        query_seg = segment_row[query_first : query_first + block_len]
        key_len = query_first + block_len
        key_part = lax.slice_in_dim(key_rows, 0, key_len, axis=0)
        value_part = lax.slice_in_dim(value_rows, 0, key_len, axis=0)
        key_seg = lax.slice_in_dim(segment_row, 0, key_len, axis=0)
        key_pos = jnp.arange(key_len, dtype=jnp.int32)
        scores = (
            jnp.einsum("qhd,khd->hqk", query_part, key_part, preferred_element_type=jnp.float32)
            * factor[:, None, None]
        )
        allowed = (query_seg[:, None] == key_seg[None, :]) & (
            key_pos[None, :] <= query_pos[:, None]
        )
        weights = jnp.where(allowed[None], jnp.exp(scores), 0.0)
        summed = jnp.einsum(
            "hqk,khd->qhd",
            weights.astype(jnp.bfloat16),
            value_part,
            preferred_element_type=jnp.float32,
        )
        summed, denominator = (summed, jnp.sum(weights, axis=-1))
        pieces.append(
            (summed / jnp.transpose(denominator)[:, :, None]).reshape(block_len, local_width)
        )
    attended = jnp.concatenate(pieces, axis=0).astype(jnp.bfloat16)
    returned = lax.all_to_all(attended, "seq", split_axis=0, concat_axis=1, tiled=True)
    branch = jnp.dot(
        returned,
        lax.all_gather(out_weight, ("dp", "seq"), axis=1, tiled=True),
        preferred_element_type=jnp.float32,
    )
    layer_out = (embedded.astype(jnp.float32) + branch).astype(jnp.bfloat16)
    grad_term = lax.dot_general(
        returned, cotangent, CONTRACT_FIRST, preferred_element_type=jnp.float32
    )
    out_grad = lax.psum_scatter(grad_term, ("dp", "seq"), scatter_dimension=1, tiled=True)
    return (layer_out, out_grad)


def solution(mesh):
    placed = (
        P(None, ("dp", "seq")),
        P("dp", None),
        P("dp", None, None),
        P(),
        P(),
        P(),
        P(),
        P(),
        P(),
        P(),
        P(),
        P(None, ("dp", "seq")),
        P(("dp", "seq"), None),
    )
    return jax.shard_map(
        per_device,
        mesh=mesh,
        in_specs=placed,
        out_specs=(P(("dp", "seq"), None), P(None, ("dp", "seq"))),
        check_vma=False,
    )
```

profile of v0, /device:TPU:2, one launch (start us, length us, event | category | flops | bytes accessed | tf_op | source)
XLA Modules:
  0.0 472.5 jit_solution(12129723158445891963)
XLA Ops:
  7.2 0.0 copy-start
  7.2 0.9 slice_bitcast_fusion.37
  8.0 0.2 select_reduce_fusion.2
  8.2 0.7 fusion.119
  8.9 0.7 fusion.118
  9.6 0.4 select_reduce_fusion.1
  10.0 0.1 compare_select_fusion.4
  10.1 2.9 scatter_custom_fusion
  13.1 0.0 copy-done
  13.1 0.0 copy-start.4
  13.1 0.0 copy-start.5
  13.1 0.0 copy-start.6
  13.1 4.2 fusion.23
  17.3 0.0 copy-done.4
  17.3 0.0 copy-done.5
  17.3 0.0 copy-done.6
  17.3 2.0 fusion.9
  19.3 1.0 concatenate.7
  20.3 6.5 %gather_fusion = bf16[768,1280]{1,0:T(8,128)(2,1)} fusion(bf16[385,1280]{1,0:T(8,128)(2,1)} %concatenate.7, s32[1024]{0:T(1024)S(1)} %pad_clamp_fusion.1), kind=kCustom, calls=%fused_computation | custom fusion | bytes 3935232 | tf_op jit(solution)/shard_map/gather | solution.py:102
  26.8 4.5 all-to-all-start
  31.3 8.2 %copy.25 = bf16[1280,3,640]{0,2,1:T(8,128)(2,1)} copy(bf16[1280,3,640]{2,0,1:T(8,128)(2,1)} %param.23) | data formatting | bytes 9830400 | tf_op args[10]
  39.5 0.1 compare_select_fusion
  39.6 11.9 %scatter_custom_fusion.1 = s32[384]{0:T(512)S(1)} fusion(s32[3072]{0:T(1024)S(1)} %bitcast.265, s32[3072]{0:T(1024)S(1)} %get-tuple-element.36, s32[]{:T(128)} %constant.25.clone.1), kind=kCustom, calls=%fused_computation.154 | custom fusion | bytes 1540 | tf_op jit(solution)/shard_map/scatter | solution.py:96
  51.6 5.6 %all-to-all-done = bf16[8,96,1280]{2,1,0:T(8,128)(2,1)} async-done(((bf16[8,96,1280]{2,1,0:T(8,128)(2,1)}), bf16[8,96,1280]{2,1,0:T(8,128)(2,1)}, u32[]{:S(2)}, u32[]{:S(2)}) %all-to-all-start) | async-done | bytes 1966112 | tf_op jit(solution)/shard_map/all_to_all | solution.py:102
  57.2 5.6 %gather_fusion.1 = bf16[384,1280]{1,0:T(8,128)(2,1)} fusion(bf16[768,1280]{1,0:T(8,128)(2,1)} %bitcast.6, s32[1024]{0:T(1024)S(1)} %pad_clamp_fusion), kind=kCustom, calls=%fused_computation.1 | custom fusion | bytes 1967616 | tf_op jit(solution)/shard_map/gather | solution.py:103
  62.8 1.5 fusion.16
  64.3 6.2 %convolution_convert_fusion = bf16[384,1920]{1,0:T(8,128)(2,1)} fusion(bf16[1280,1920]{0,1:T(8,128)(2,1)} %bitcast.255, bf16[384,1280]{1,0:T(8,128)(2,1)} %gather_fusion.1, f32[1280]{0:T(1024)S(1)} %copy-done.7, f32[384]{0:T(512)S(1)} %add_rsqrt_fusion.2), kind=kOutput, calls=%fused_computation.27 | convolution fusion | flops 1890140160 | bytes 7379456 | tf_op jit(solution)/shard_map/dot_general | solution.py:105
  70.5 2.6 copy.26
  73.0 3.9 copy.27
  77.0 4.5 all-to-all-start.1
  81.4 0.0 all-gather.3.cloned.1.call-start
  81.5 0.7 all-gather.3.cloned.1.call-update
  82.2 0.3 all-reduce.4.cloned.1.call-start
  82.4 0.6 dynamic_slice.11
  83.8 23.4 %all-to-all-done.1 = bf16[384,3,640]{0,1,2:T(4,128)(2,1)} async-done(((bf16[384,3,640]{0,1,2:T(4,128)(2,1)}), bf16[384,3,640]{0,1,2:T(4,128)(2,1)}, u32[]{:S(2)}, u32[]{:S(2)}) %all-to-all-start.1) | async-done | bytes 1474592 | tf_op jit(solution)/shard_map/all_to_all | solution.py:109
  107.3 1.7 copy.28
  109.0 0.3 copy.32
  109.3 0.2 fusion.94
  109.5 0.2 fusion.95
  109.7 0.0 slice-start
  109.7 0.4 fusion.121
  110.2 0.2 fusion.91
  110.4 0.0 slice-done
  110.4 0.9 fusion.122
  111.4 1.4 fusion.123
  112.7 0.5 fusion.87
  113.2 0.6 fusion.63
  113.8 1.9 fusion.124
  115.7 0.8 fusion.81
  116.5 2.3 fusion.125
  118.8 0.9 fusion.75
  119.8 2.7 fusion.126
  122.5 0.0 copy-start.2
  122.5 1.1 fusion.69
  123.6 0.1 copy.34
  123.6 12.4 %all_to_all.46 = bf16[8,384,80]{1,2,0:T(8,128)(2,1)S(1)} all-to-all(bf16[8,384,80]{1,2,0:T(8,128)(2,1)S(1)} %bitcast.258), channel_id=1, replica_groups=mesh['dp'=32,'seq'=8] {'seq'}, dimensions={0} | all-to-all | bytes 983040 | tf_op jit(solution)/shard_map/all_to_all | solution.py:155
  136.1 0.8 copy-done.1
  136.9 2.9 fusion.127
  139.7 0.0 all-reduce.4.cloned.1.call-update
  139.7 54.4 %all-gather.3.cloned.1.call-done = bf16[256,5,640]{2,1,0:T(8,128)(2,1)} async-done(((bf16[1,5,640]{2,1,0:T(8,128)(2,1)}), bf16[256,5,640]{2,1,0:T(8,128)(2,1)}) %all-gather.3.cloned.1.call-update) | async-done | bytes 1638416 | tf_op jit(solution)/shard_map/all_gather | solution.py:158
  194.1 4.1 reshape.456
  198.2 3.8 fusion.10
  202.0 262.3 %all-reduce.4.cloned.1.call-done = f32[640,1280]{0,1:T(8,128)} async-done(((f32[640,1280]{0,1:T(8,128)}), f32[640,1280]{0,1:T(8,128)}) %all-reduce.4.cloned.1.call-update) | async-done | bytes 3276816
  464.3 1.4 constant_dynamic-slice_fusion
  (28 shorter events, 0.2 us)
Async XLA Ops:
  7.2 5.9 %copy-start = (bf16[1280,1280]{1,0:T(8,128)(2,1)S(1)}, bf16[1280,1280]{1,0:T(8,128)(2,1)}, u32[]{:S(2)}) copy-start(bf16[1280,1280]{1,0:T(8,128)(2,1)} %param.19) | copy-start | bytes 9830404
  13.1 4.2 copy-start.4
  13.1 4.2 copy-start.5
  13.1 4.2 copy-start.6
  26.8 30.4 %all-to-all-start = ((bf16[8,96,1280]{2,1,0:T(8,128)(2,1)}), bf16[8,96,1280]{2,1,0:T(8,128)(2,1)}, u32[]{:S(2)}, u32[]{:S(2)}) async-start(bf16[8,96,1280]{2,1,0:T(8,128)(2,1)} %bitcast.252), calls=%async_computation | async-start | bytes 3932160 | tf_op jit(solution)/shard_map/all_to_all | solution.py:102
  57.2 7.1 %copy-start.7 = (f32[1280]{0:T(1024)S(1)}, f32[1280]{0:T(1024)}, u32[]{:S(2)}) copy-start(f32[1280]{0:T(1024)} %param.21) | copy-start | bytes 15364
  76.9 5.5 %copy-start.8 = (f32[8]{0:T(128)S(1)}, f32[8]{0:T(128)}, u32[]{:S(2)}) copy-start(f32[8]{0:T(128)} %param.22) | copy-start | bytes 100
  76.9 6.8 %copy-start.3 = (s32[1,3072]{1,0:T(1,128)S(1)}, s32[1,3072]{1,0:T(1,128)}, u32[]{:S(2)}) copy-start(s32[1,3072]{1,0:T(1,128)} %param.14) | copy-start | bytes 36868
  77.0 30.3 %all-to-all-start.1 = ((bf16[384,3,640]{0,1,2:T(4,128)(2,1)}), bf16[384,3,640]{0,1,2:T(4,128)(2,1)}, u32[]{:S(2)}, u32[]{:S(2)}) async-start(bf16[384,3,640]{0,1,2:T(4,128)(2,1)} %copy.27), calls=%async_computation.1 | async-start | bytes 3932160 | tf_op jit(solution)/shard_map/all_to_all | solution.py:109
  81.4 112.7 %all-gather.3.cloned.1.call-start = ((), (), s32[]{:S(2)}) async-start(), calls=%async_computation.3 | async-start | bytes 2631680 | tf_op jit(solution)/shard_map/all_gather | solution.py:158
  82.2 382.1 %all-reduce.4.cloned.1.call-start = ((), (), s32[]{:S(2)}) async-start(), calls=%async_computation.4 | async-start | bytes 6553600
  109.7 0.7 slice-start
  112.7 1.1 slice-start.1
  122.5 14.4 %copy-start.2 = (bf16[384,1280]{1,0:T(8,128)(2,1)S(1)}, bf16[384,1280]{1,0:T(8,128)(2,1)}, u32[]{:S(2)}) copy-start(bf16[384,1280]{1,0:T(8,128)(2,1)} %param.25) | copy-start | bytes 2949124
  136.1 0.8 copy-start.1
Sparse Core Ops, SparseCore 0:
  86.0 108.0 all-gather.2
  199.6 264.6 all-reduce.3
where the time goes:
time: 474 us; the launch traced here: 473 us
  waiting for transfers between devices  346 us (73%)
  local copies, waits for them, and re-layouts  52.6 us (11%)
  matrix products  32.7 us (7%)
  between operations  15 us (3%)
  blocking collectives  12.4 us (3%)
  starting transfers between devices  9.23 us (2%)
    unnamed x3, waiting for transfers between devices  263 us
    all_gather x1, waiting for transfers between devices, per_device(): lax.all_gather(out_weight, ('dp', 'seq'), axis=1, tiled=True)  54.4 us
    all_to_all x1, waiting for transfers between devices, per_device(): lax.all_to_all(projected, 'seq', split_axis=2, concat_axis=0, tiled=True)  23.4 us
    unnamed x21, local copies, waits for them, and re-layouts  14.5 us
    all_to_all x1, blocking collectives, per_device(): lax.all_to_all(attended, 'seq', split_axis=0, concat_axis=1, tiled=True)  12.4 us
    scatter x1, local copies, waits for them, and re-layouts, per_device(): receive_table = jnp.zeros((shard_rows,), jnp.int32).at[landing].set(loade...  11.9 us
    dot_general x6, matrix products, per_device(): jnp.einsum('qhd,khd->hqk', query_part, key_part, preferred_element_type=j...  9.69 us
  transfers between devices with their start and end apart: 4, of which 4 were waited for; matrix products, arithmetic and copies ran while one was open for 10% of the time, Pallas kernels for 0%

commit v1 on v0

--- a/solution.py
+++ b/solution.py
@@ -7,6 +7,28 @@
 HD = 80
 EPSILON = 1e-06
 CONTRACT_FIRST = (((0,), (0,)), ((), ()))
+
+
+def split_up(array, dim, size):
+    before, after = (array.shape[:dim], array.shape[dim + 1 :])
+    return jnp.moveaxis(array.reshape(*before, size, -1, *after), dim, 0)
+
+
+def joined_along(blocks, dim):
+    shape = list(blocks.shape[1:])
+    shape[dim] *= blocks.shape[0]
+    return jnp.moveaxis(blocks, 0, dim).reshape(shape)
+
+
+def pairwise_exchange(value, axis, split_dim, concat_dim):
+    length, position = (lax.axis_size(axis), lax.axis_index(axis))
+    pieces = split_up(value, split_dim, length)
+    outs = [pieces[position]]
+    for step in range(1, length):
+        sent = pieces[position ^ step]
+        outs.append(lax.ppermute(sent, axis, [(i, i ^ step) for i in range(length)]))
+    pieces = jnp.stack(outs)[position ^ jnp.arange(length)]
+    return joined_along(pieces, concat_dim)
 
 
 def row_norm(values):
@@ -106,7 +128,7 @@
         normed, qkv_weight.reshape(model_width, -1), preferred_element_type=jnp.float32
     )
     projected = projected.astype(jnp.bfloat16).reshape(shard_rows, 3, -1)
-    head_rows = lax.all_to_all(projected, "seq", split_axis=2, concat_axis=0, tiled=True)
+    head_rows = pairwise_exchange(projected, "seq", 2, 0)
     local_width = head_rows.shape[2]
     local_heads = local_width // HD
     queries = row_norm(

time: 474 us -> 428 us (0.903)
  waiting for transfers between devices: 346 us -> 290 us
  local copies, waits for them, and re-layouts: 52.6 us -> 59.3 us
    all_gather x1, waiting for transfers between devices: 54.4 us -> 9.75 us  [per_device(): lax.all_gather(out_weight, ('dp', 'seq'), axis=1, tiled=True)]
    all_to_all x1 -> x0, waiting for transfers between devices: 23.4 us -> none  [per_device(): lax.all_to_all(projected, 'seq', split_axis=2, concat_axis=0, tiled=True)]
    ppermute x0 -> x7, waiting for transfers between devices: none -> 13 us  [pairwise_exchange(): lax.ppermute(sent, axis, [(i, i ^ step) for i in range(length)])]
    ppermute x0 -> x7, starting transfers between devices: none -> 8.14 us  [pairwise_exchange(): lax.ppermute(sent, axis, [(i, i ^ step) for i in range(length)])]
    unnamed x21 -> x28, local copies, waits for them, and re-layouts: 14.5 us -> 20.3 us
  transfers between devices with their start and end apart: 4 -> 10, of which waited for: 4 -> 7; matrix products, arithmetic and copies ran while one was open for 10% -> 17% of each run, Pallas kernels for 0% -> 0%
where the time goes in v1:
time: 428 us; the launch traced here: 427 us
  waiting for transfers between devices  290 us (68%)
  local copies, waits for them, and re-layouts  59.3 us (14%)
  matrix products  32.7 us (8%)
  between operations  15.1 us (4%)
  blocking collectives  13.5 us (3%)
  starting transfers between devices  12.7 us (3%)
    unnamed x3, waiting for transfers between devices  263 us
    unnamed x28, local copies, waits for them, and re-layouts  20.3 us
    all_to_all x1, blocking collectives, per_device(): lax.all_to_all(attended, 'seq', split_axis=0, concat_axis=1, tiled=True)  13.5 us
    ppermute x7, waiting for transfers between devices, pairwise_exchange(): lax.ppermute(sent, axis, [(i, i ^ step) for i in range(length)])  13 us
    scatter x1, local copies, waits for them, and re-layouts, per_device(): receive_table = jnp.zeros((shard_rows,), jnp.int32).at[landing].set(loade...  11.8 us
    all_gather x1, waiting for transfers between devices, per_device(): lax.all_gather(out_weight, ('dp', 'seq'), axis=1, tiled=True)  9.75 us
    dot_general x6, matrix products, per_device(): jnp.einsum('qhd,khd->hqk', query_part, key_part, preferred_element_type=j...  9.69 us
  transfers between devices with their start and end apart: 10, of which 7 were waited for; matrix products, arithmetic and copies ran while one was open for 17% of the time, Pallas kernels for 0%

profile of v1, /device:TPU:2, one launch (start us, length us, event | category | flops | bytes accessed | tf_op | source)
XLA Modules:
  0.0 427.0 jit_solution(4654660891417229234)
XLA Ops:
  7.2 0.9 slice_bitcast_fusion.37
  8.0 0.2 select_reduce_fusion.2
  8.2 0.7 fusion.120
  8.9 0.7 fusion.119
  9.6 0.4 select_reduce_fusion.1
  10.0 0.1 compare_select_fusion.4
  10.1 2.9 scatter_custom_fusion
  13.1 4.2 fusion.23
  17.3 2.0 fusion.9
  19.3 1.0 concatenate.7
  20.3 6.5 %gather_fusion = bf16[768,1280]{1,0:T(8,128)(2,1)} fusion(bf16[385,1280]{1,0:T(8,128)(2,1)} %concatenate.7, s32[1024]{0:T(1024)S(1)} %pad_clamp_fusion.2), kind=kCustom, calls=%fused_computation | custom fusion | bytes 3935232 | tf_op jit(solution)/shard_map/gather | solution.py:124
  26.8 4.5 %all-to-all-start = ((bf16[8,96,1280]{2,1,0:T(8,128)(2,1)}), bf16[8,96,1280]{2,1,0:T(8,128)(2,1)}, u32[]{:S(2)}, u32[]{:S(2)}) async-start(bf16[8,96,1280]{2,1,0:T(8,128)(2,1)} %bitcast.282), calls=%async_computation | async-start | bytes 3932160 | tf_op jit(solution)/shard_map/all_to_all | solution.py:124
  31.4 0.7 all-gather.3.cloned.1.call-update
  32.3 8.2 %copy.26 = bf16[1280,3,640]{0,2,1:T(8,128)(2,1)} copy(bf16[1280,3,640]{2,0,1:T(8,128)(2,1)} %param.23) | data formatting | bytes 9830400 | tf_op args[10]
  40.5 0.6 dynamic_slice.22
  41.7 11.8 %scatter_custom_fusion.1 = s32[384]{0:T(512)S(1)} fusion(s32[3072]{0:T(1024)S(1)} %bitcast.295, s32[3072]{0:T(1024)S(1)} %get-tuple-element.43, s32[]{:T(128)} %constant.31.clone.1), kind=kCustom, calls=%fused_computation.172 | custom fusion | bytes 1540 | tf_op jit(solution)/shard_map/scatter | solution.py:118
  53.7 3.6 all-to-all-done
  57.3 5.6 %gather_fusion.1 = bf16[384,1280]{1,0:T(8,128)(2,1)} fusion(bf16[768,1280]{1,0:T(8,128)(2,1)} %bitcast.6, s32[1024]{0:T(1024)S(1)} %pad_clamp_fusion.1), kind=kCustom, calls=%fused_computation.1 | custom fusion | bytes 1967616 | tf_op jit(solution)/shard_map/gather | solution.py:125
  62.9 1.5 fusion.16
  64.3 6.1 %convolution_convert_fusion = bf16[384,1920]{1,0:T(8,128)(2,1)} fusion(bf16[1280,1920]{0,1:T(8,128)(2,1)} %bitcast.285, bf16[384,1280]{1,0:T(8,128)(2,1)} %gather_fusion.1, f32[1280]{0:T(1024)S(1)} %copy-done.7, f32[384]{0:T(512)S(1)} %add_rsqrt_fusion.2), kind=kOutput, calls=%fused_computation.28 | convolution fusion | flops 1890140160 | bytes 7379456 | tf_op jit(solution)/shard_map/dot_general | solution.py:127
  70.5 2.6 copy.27
  73.0 1.5 dynamic-slice_bitcast_fusion
  74.6 0.8 collective-permute-start.1
  75.5 1.0 collective-permute-start.2
  76.5 1.1 collective-permute-start.3
  77.5 2.4 collective-permute-start.4
  79.9 1.6 bitcast_dynamic-update-slice_fusion.7
  81.5 1.2 collective-permute-start.5
  82.7 0.7 bitcast_dynamic-update-slice_fusion.6
  83.4 1.6 collective-permute-start.6
  85.0 0.7 bitcast_dynamic-update-slice_fusion.5
  85.7 0.7 bitcast_dynamic-update-slice_fusion.4
  86.4 4.7 %collective-permute-done.3 = bf16[384,3,80]{0,2,1:T(8,128)(2,1)S(1)} collective-permute-done((bf16[384,3,80]{0,2,1:T(8,128)(2,1)S(1)}, bf16[384,3,80]{0,2,1:T(8,128)(2,1)S(1)}, u32[]{:S(2)}, u32[]{:S(2)}) %collective-permute-start.3) | collective-permute-done | bytes 184352 | tf_op jit(solution)/shard_map/ppermute | solution.py:29
  91.2 0.7 bitcast_dynamic-update-slice_fusion.3
  91.9 1.8 collective-permute-done.4
  93.7 0.7 bitcast_dynamic-update-slice_fusion.2
  94.4 3.7 collective-permute-done.5
  98.1 0.7 bitcast_dynamic-update-slice_fusion.1
  98.8 2.8 collective-permute-done.6
  101.5 0.7 bitcast_dynamic-update-slice_fusion
  102.2 3.2 gather_fusion.2
  105.5 1.6 copy.31
  107.1 0.2 fusion.94
  107.4 0.2 fusion.95
  107.6 0.4 fusion.122
  108.0 0.2 fusion.91
  108.2 0.9 fusion.123
  109.2 1.4 fusion.124
  110.5 0.5 fusion.87
  111.0 0.6 fusion.63
  111.6 1.9 fusion.125
  113.6 0.8 fusion.81
  114.3 2.3 fusion.126
  116.7 0.9 fusion.75
  117.6 2.7 fusion.127
  120.3 1.1 fusion.69
  121.4 13.5 %all_to_all.28 = bf16[8,384,80]{1,2,0:T(8,128)(2,1)S(1)} all-to-all(bf16[8,384,80]{1,2,0:T(8,128)(2,1)S(1)} %bitcast.288), channel_id=1, replica_groups=mesh['dp'=32,'seq'=8] {'seq'}, dimensions={0} | all-to-all | bytes 983040 | tf_op jit(solution)/shard_map/all_to_all | solution.py:177
  134.9 0.8 copy-done.1
  135.7 2.9 fusion.128
  138.6 9.7 %all-gather.3.cloned.1.call-done = bf16[256,5,640]{2,1,0:T(8,128)(2,1)} async-done(((bf16[1,5,640]{2,1,0:T(8,128)(2,1)}), bf16[256,5,640]{2,1,0:T(8,128)(2,1)}) %all-gather.3.cloned.1.call-update) | async-done | bytes 1638416 | tf_op jit(solution)/shard_map/all_gather | solution.py:180
  148.4 4.1 reshape.495
  152.5 3.8 fusion.10
  156.2 262.6 %all-reduce.4.cloned.1.call-done = f32[640,1280]{0,1:T(8,128)} async-done(((f32[640,1280]{0,1:T(8,128)}), f32[640,1280]{0,1:T(8,128)}) %all-reduce.4.cloned.1.call-update) | async-done | bytes 3276816
  418.8 1.4 constant_dynamic-slice_fusion
  (50 shorter events, 0.6 us)
Async XLA Ops:
  7.2 5.9 %copy-start = (bf16[1280,1280]{1,0:T(8,128)(2,1)S(1)}, bf16[1280,1280]{1,0:T(8,128)(2,1)}, u32[]{:S(2)}) copy-start(bf16[1280,1280]{1,0:T(8,128)(2,1)} %param.19) | copy-start | bytes 9830404
  13.1 4.2 copy-start.4
  13.1 4.2 copy-start.5
  13.1 4.2 copy-start.6
  26.8 30.4 %all-to-all-start = ((bf16[8,96,1280]{2,1,0:T(8,128)(2,1)}), bf16[8,96,1280]{2,1,0:T(8,128)(2,1)}, u32[]{:S(2)}, u32[]{:S(2)}) async-start(bf16[8,96,1280]{2,1,0:T(8,128)(2,1)} %bitcast.282), calls=%async_computation | async-start | bytes 3932160 | tf_op jit(solution)/shard_map/all_to_all | solution.py:124
  31.3 117.1 %all-gather.3.cloned.1.call-start = ((), (), s32[]{:S(2)}) async-start(), calls=%async_computation.2 | async-start | bytes 2631680 | tf_op jit(solution)/shard_map/all_gather | solution.py:180
  32.0 386.8 %all-reduce.4.cloned.1.call-start = ((), (), s32[]{:S(2)}) async-start(), calls=%async_computation.3 | async-start | bytes 6553600
  32.2 8.2 %copy-start.8 = (f32[8]{0:T(128)S(1)}, f32[8]{0:T(128)}, u32[]{:S(2)}) copy-start(f32[8]{0:T(128)} %param.22) | copy-start | bytes 100
  32.2 21.4 %copy-start.3 = (s32[1,3072]{1,0:T(1,128)S(1)}, s32[1,3072]{1,0:T(1,128)}, u32[]{:S(2)}) copy-start(s32[1,3072]{1,0:T(1,128)} %param.14) | copy-start | bytes 36868
  57.2 7.1 %copy-start.7 = (f32[1280]{0:T(1024)S(1)}, f32[1280]{0:T(1024)}, u32[]{:S(2)}) copy-start(f32[1280]{0:T(1024)} %param.21) | copy-start | bytes 15364
  74.5 7.0 %collective-permute-start = (bf16[384,3,80]{0,2,1:T(8,128)(2,1)S(1)}, bf16[384,3,80]{0,2,1:T(8,128)(2,1)S(1)}, u32[]{:S(2)}, u32[]{:S(2)}) collective-permute-start(bf16[384,3,80]{0,2,1:T(8,128)(2,1)S(1)} %get-tuple-element.16), channel_id=1, source_target_pairs={{0,1},{1,0},{2,3},{3,2},{4,5},{5,4},{6,7},{7,6},{8,9},{9,8},{10,11... | collective-permute-start | bytes 552968 | tf_op jit(solution)/shard_map/ppermute | solution.py:29
  74.6 8.7 %collective-permute-start.1 = (bf16[384,3,80]{0,2,1:T(8,128)(2,1)S(1)}, bf16[384,3,80]{0,2,1:T(8,128)(2,1)S(1)}, u32[]{:S(2)}, u32[]{:S(2)}) collective-permute-start(bf16[384,3,80]{0,2,1:T(8,128)(2,1)S(1)} %get-tuple-element.15), channel_id=1, source_target_pairs={{0,2},{1,3},{2,0},{3,1},{4,6},{5,7},{6,4},{7,5},{8,10},{9,11},{10,... | collective-permute-start | bytes 552968 | tf_op jit(solution)/shard_map/ppermute | solution.py:29
  75.5 10.2 %collective-permute-start.2 = (bf16[384,3,80]{0,2,1:T(8,128)(2,1)S(1)}, bf16[384,3,80]{0,2,1:T(8,128)(2,1)S(1)}, u32[]{:S(2)}, u32[]{:S(2)}) collective-permute-start(bf16[384,3,80]{0,2,1:T(8,128)(2,1)S(1)} %get-tuple-element.14), channel_id=1, source_target_pairs={{0,3},{1,2},{2,1},{3,0},{4,7},{5,6},{6,5},{7,4},{8,11},{9,10},{10,... | collective-permute-start | bytes 552968 | tf_op jit(solution)/shard_map/ppermute | solution.py:29
  76.5 14.7 %collective-permute-start.3 = (bf16[384,3,80]{0,2,1:T(8,128)(2,1)S(1)}, bf16[384,3,80]{0,2,1:T(8,128)(2,1)S(1)}, u32[]{:S(2)}, u32[]{:S(2)}) collective-permute-start(bf16[384,3,80]{0,2,1:T(8,128)(2,1)S(1)} %get-tuple-element.13), channel_id=1, source_target_pairs={{0,4},{1,5},{2,6},{3,7},{4,0},{5,1},{6,2},{7,3},{8,12},{9,13},{10,... | collective-permute-start | bytes 552968 | tf_op jit(solution)/shard_map/ppermute | solution.py:29
  77.5 16.1 %collective-permute-start.4 = (bf16[384,3,80]{0,2,1:T(8,128)(2,1)S(1)}, bf16[384,3,80]{0,2,1:T(8,128)(2,1)S(1)}, u32[]{:S(2)}, u32[]{:S(2)}) collective-permute-start(bf16[384,3,80]{0,2,1:T(8,128)(2,1)S(1)} %get-tuple-element.12), channel_id=1, source_target_pairs={{0,5},{1,4},{2,7},{3,6},{4,1},{5,0},{6,3},{7,2},{8,13},{9,12},{10,... | collective-permute-start | bytes 552968 | tf_op jit(solution)/shard_map/ppermute | solution.py:29
  81.5 16.5 %collective-permute-start.5 = (bf16[384,3,80]{0,2,1:T(8,128)(2,1)S(1)}, bf16[384,3,80]{0,2,1:T(8,128)(2,1)S(1)}, u32[]{:S(2)}, u32[]{:S(2)}) collective-permute-start(bf16[384,3,80]{0,2,1:T(8,128)(2,1)S(1)} %get-tuple-element.11), channel_id=1, source_target_pairs={{0,6},{1,7},{2,4},{3,5},{4,2},{5,3},{6,0},{7,1},{8,14},{9,15},{10,... | collective-permute-start | bytes 552968 | tf_op jit(solution)/shard_map/ppermute | solution.py:29
  83.4 18.1 %collective-permute-start.6 = (bf16[384,3,80]{0,2,1:T(8,128)(2,1)S(1)}, bf16[384,3,80]{0,2,1:T(8,128)(2,1)S(1)}, u32[]{:S(2)}, u32[]{:S(2)}) collective-permute-start(bf16[384,3,80]{0,2,1:T(8,128)(2,1)S(1)} %get-tuple-element.10), channel_id=1, source_target_pairs={{0,7},{1,6},{2,5},{3,4},{4,3},{5,2},{6,1},{7,0},{8,15},{9,14},{10,... | collective-permute-start | bytes 552968 | tf_op jit(solution)/shard_map/ppermute | solution.py:29
  107.5 0.7 slice-start
  110.5 1.1 slice-start.1
  120.3 15.4 %copy-start.2 = (bf16[384,1280]{1,0:T(8,128)(2,1)S(1)}, bf16[384,1280]{1,0:T(8,128)(2,1)}, u32[]{:S(2)}) copy-start(bf16[384,1280]{1,0:T(8,128)(2,1)} %param.25) | copy-start | bytes 2949124
  134.9 0.8 copy-start.1
Sparse Core Ops, SparseCore 0:
  35.9 112.4 all-gather.2
  153.9 264.8 all-reduce.3
